TPU v7x, 32 devices: a whole 2x2x4 slice. The times are simulated.
32 devices in a mesh: space: 8 (over z, y), sub: 4 (over x, core).
Axes of the slice: x: 2, y: 2, z: 4, core: 2. Of those that a mesh axis runs over, the one named last changes fastest.
Arguments:
- rhs: bfloat16 [4096, 1024], P(('space', 'sub')), may hold values from -6 to 6
- blocks: bfloat16 [4096, 7, 4096], P(('space', 'sub')), may hold values from -0.125 to 0.125
- columns: int32 [4096, 7], P(('space', 'sub')), may hold values from 0 to 639, as said below
- ghost_lists: int32 [32, 128], P(('space', 'sub')), may hold values from 0 to 127, as said below
Outputs:
- solution: float32 [4096, 1024], P(('space', 'sub'))
- residual: float32 [4096, 1024], P(('space', 'sub'))
Inputs may be any that keep to these rules, and one draw needn't show every extreme that they name: `columns`: for block row r (local) of device (p, q): entry 0 is q * 128 + r; entries 1 and 2 are q2 * 128 + ghost_lists[p * 4 + q2, k] for some q2 < 4 and k < 64; entries 3 and 4 lie in the part received from the previous subdomain, entries 5 and 6 in that from the next. `ghost_lists`: each row is a permutation of 0 .. 127.
All inputs are finite; a program needn't handle non-finite values.
Results may differ from a plain program's by a relative error of at most 0.0055.
Values may be sent and summed in bfloat16 or wider, within the bound.
A program may use at most 128 MiB of HBM per device.

v0:
```python
import jax
import jax.numpy as jnp
from jax import lax
from jax.sharding import PartitionSpec as P

BS = 64
NRHS = 16
NNZ = 7
S = 4


def shifted(value, axis, steps):
    count = lax.axis_size(axis)
    initial, last = (max(0, -steps), min(count, count - steps))
    return lax.ppermute(value, axis, [(source, source + steps) for source in range(initial, last)])


def finish(rhs, stack, gram):
    rows = stack.shape[0]
    paired = gram[1:] + gram[:-1]
    hmat = (paired[:, :, 1:] + paired[:, :, :-1]).reshape(S * NRHS, S * NRHS)
    cvec = paired[:, :, 0].reshape(S * NRHS, NRHS)
    lower = jnp.linalg.cholesky(hmat)
    coef = jax.scipy.linalg.cho_solve((lower, True), cvec).reshape(S, NRHS, NRHS)
    kfull = stack.astype(jnp.float32)
    highest = lax.Precision.HIGHEST
    sol = jnp.einsum("rjia,jac->ric", kfull[:, :S], coef, precision=highest)
    wmat = kfull[:, 1:] + kfull[:, :S]
    image = jnp.einsum("rjia,jac->ric", wmat, coef, precision=highest)
    res = rhs.astype(jnp.float32).reshape(rows, BS, NRHS) - image
    return (sol.reshape(rows, BS * NRHS), res.reshape(rows, BS * NRHS))


def on_device(rhs, blocks, columns, ghost_lists):
    rows = rhs.shape[0]
    ghost = ghost_lists.shape[1] // 2
    send_up = ghost_lists[0, :ghost]
    send_down = ghost_lists[0, ghost:]
    mats = blocks.reshape(rows, NNZ, BS, BS)
    basis = [rhs]
    for j in range(S):
        current = basis[-1]
        boundary = current[send_up]
        lower = shifted(boundary, "space", 1)
        upper = shifted(current[send_down], "space", -1)
        whole = lax.all_gather(current, "sub", axis=0, tiled=True)
        extended = jnp.concatenate([whole, lower, upper], axis=0)
        picked = extended[columns].reshape(rows, NNZ, BS, NRHS)
        nxt = jnp.einsum("rbij,rbjk->rik", mats, picked, preferred_element_type=jnp.float32)
        basis.append(nxt.astype(jnp.bfloat16).reshape(rows, BS * NRHS))
    stack = jnp.stack(basis, axis=1).reshape(rows, S + 1, BS, NRHS)
    partial_value = jnp.einsum("rjia,rkic->jakc", stack, stack, preferred_element_type=jnp.float32)
    gram = lax.psum(partial_value, ("space", "sub"))
    return finish(rhs, stack, gram)


def solution(mesh):
    in_specs = (
        P(("space", "sub"), None),
        P(("space", "sub"), None, None),
        P(("space", "sub"), None),
        P(("space", "sub"), None),
    )
    out_specs = (P(("space", "sub"), None), P(("space", "sub"), None))
    return jax.shard_map(
        on_device, mesh=mesh, in_specs=in_specs, out_specs=out_specs, check_vma=False
    )
```

profile of v0, /device:TPU:0, one launch (start us, length us, event | category | flops | bytes accessed | tf_op | source)
XLA Modules:
  0.0 319.2 jit_solution(4314674499148985406)
XLA Ops:
  7.2 0.7 all-gather.5.cloned.1.call-update
  8.0 0.8 fusion.27
  8.8 1.8 gather_fusion
  10.6 4.9 %collective-permute-start = (bf16[64,1024]{1,0:T(8,128)(2,1)S(1)}, bf16[64,1024]{1,0:T(8,128)(2,1)S(1)}, u32[]{:S(2)}, u32[]{:S(2)}) collective-permute-start(bf16[64,1024]{1,0:T(8,128)(2,1)S(1)} %gather_fusion), channel_id=1, source_target_pairs={{0,4},{4,8},{8,12},{12,16},{16,20},{20,24},{24,28},{1,5},{5,9},{9,... | collective-permute-start | bytes 393224 | tf_op jit(solution)/shard_map/ppermute | solution.py:15
  15.5 1.8 gather_fusion.1
  17.2 1.3 collective-permute-start.1
  19.1 10.9 %copy.27 = bf16[128,7,4096]{0,2,1:T(8,128)(2,1)} copy(bf16[128,7,4096]{2,0,1:T(8,128)(2,1)} %param.5) | data formatting | bytes 14680064 | tf_op args[1]
  30.0 21.2 %copy.29 = bf16[128,7,64,64]{3,2,1,0:T(8,128)(2,1)} copy(bf16[128,7,64,64]{0,3,2,1:T(8,128)(2,1)} %bitcast.114) | data formatting | bytes 14680064 | tf_op jit(solution)/shard_map/reshape | solution.py:39
  51.7 1.0 constant_dynamic-update-slice_fusion.3
  52.8 1.3 pad_maximum_fusion
  54.1 3.6 %gather_fusion.2 = bf16[896,1024]{1,0:T(8,128)(2,1)S(1)} fusion(bf16[640,1024]{1,0:T(8,128)(2,1)S(1)} %pad_maximum_fusion, s32[1024]{0:T(1024)S(1)} %pad_clamp_fusion), kind=kCustom, calls=%fused_computation.2 | custom fusion | bytes 3673600 | tf_op jit(solution)/shard_map/gather | solution.py:48
  57.7 13.8 %reshape.125 = bf16[128,7,64,16]{3,2,1,0:T(8,128)(2,1)} reshape(bf16[896,1024]{1,0:T(8,128)(2,1)S(1)} %gather_fusion.2) | data formatting | bytes 3670016 | tf_op jit(solution)/shard_map/reshape | solution.py:48
  71.5 12.5 %constant_dynamic-update-slice_fusion.2 = (bf16[128,5,64,16]{2,3,0,1:T(8,128)(2,1)}, bf16[128,16,64]{2,1,0:T(8,128)(2,1)S(1)}) fusion(bf16[128,5,64,16]{2,3,0,1:T(8,128)(2,1)} %constant_dynamic-update-slice_fusion.3, bf16[128,7,64,16]{3,2,1,0:T(8,128)(2,1)} %reshape.125, bf16[128,7,64,64]{3,2,1,0:T(8,128)(2,1)} %copy.29), kind=kOutput, calls=%fused_computation.57 | convolution fusion | flops 117571584 | bytes 30146560 | tf_op jit(solution)/shard_map/rbij,rbjk->rik/dot_general | solution.py:49
  84.1 0.6 copy.30
  84.7 0.9 copy.31
  85.6 1.8 gather_fusion.3
  87.4 1.8 gather_fusion.4
  89.2 4.4 %collective-permute-start.2 = (bf16[64,1024]{1,0:T(8,128)(2,1)S(1)}, bf16[64,1024]{1,0:T(8,128)(2,1)S(1)}, u32[]{:S(2)}, u32[]{:S(2)}) collective-permute-start(bf16[64,1024]{1,0:T(8,128)(2,1)S(1)} %gather_fusion.3), channel_id=1, source_target_pairs={{0,4},{4,8},{8,12},{12,16},{16,20},{20,24},{24,28},{1,5},{5,9},{9,... | collective-permute-start | bytes 393224 | tf_op jit(solution)/shard_map/ppermute | solution.py:15
  93.6 1.5 collective-permute-start.3
  95.1 1.0 collective-permute-done.2
  96.1 4.8 %collective-permute-done.3 = bf16[64,1024]{1,0:T(8,128)(2,1)S(1)} collective-permute-done((bf16[64,1024]{1,0:T(8,128)(2,1)S(1)}, bf16[64,1024]{1,0:T(8,128)(2,1)S(1)}, u32[]{:S(2)}, u32[]{:S(2)}) %collective-permute-start.3) | collective-permute-done | bytes 131104 | tf_op jit(solution)/shard_map/ppermute | solution.py:15
  100.8 3.8 %all-gather.7.cloned.1.call-done = bf16[512,1024]{1,0:T(8,128)(2,1)} async-done(((bf16[128,1024]{1,0:T(8,128)(2,1)}), bf16[512,1024]{1,0:T(8,128)(2,1)}) %all-gather.7.cloned.1.call-update) | async-done | bytes 1048592 | tf_op jit(solution)/shard_map/all_gather | solution.py:46
  104.6 1.3 pad_maximum_fusion.1
  106.0 3.6 %gather_fusion.5 = bf16[896,1024]{1,0:T(8,128)(2,1)S(1)} fusion(bf16[640,1024]{1,0:T(8,128)(2,1)S(1)} %pad_maximum_fusion.1, s32[1024]{0:T(1024)S(1)} %pad_clamp_fusion), kind=kCustom, calls=%fused_computation.5 | custom fusion | bytes 3673600 | tf_op jit(solution)/shard_map/gather | solution.py:48
  109.6 13.8 %reshape.128 = bf16[128,7,64,16]{3,2,1,0:T(8,128)(2,1)} reshape(bf16[896,1024]{1,0:T(8,128)(2,1)S(1)} %gather_fusion.5) | data formatting | bytes 3670016 | tf_op jit(solution)/shard_map/reshape | solution.py:48
  123.4 12.5 %constant_dynamic-update-slice_fusion.1 = (bf16[128,5,64,16]{2,3,0,1:T(8,128)(2,1)}, bf16[128,16,64]{2,1,0:T(8,128)(2,1)S(1)}) fusion(bf16[128,5,64,16]{2,3,0,1:T(8,128)(2,1)} %get-tuple-element.8, bf16[128,7,64,16]{3,2,1,0:T(8,128)(2,1)} %reshape.128, bf16[128,7,64,64]{3,2,1,0:T(8,128)(2,1)} %copy.29), kind=kOutput, calls=%fused_computation.56 | convolution fusion | flops 117571584 | bytes 30146560 | tf_op jit(solution)/shard_map/rbij,rbjk->rik/dot_general | solution.py:49
  135.9 0.6 copy.36
  136.5 0.9 copy.37
  137.5 1.8 gather_fusion.6
  139.2 1.8 gather_fusion.7
  141.0 3.4 %collective-permute-start.4 = (bf16[64,1024]{1,0:T(8,128)(2,1)S(1)}, bf16[64,1024]{1,0:T(8,128)(2,1)S(1)}, u32[]{:S(2)}, u32[]{:S(2)}) collective-permute-start(bf16[64,1024]{1,0:T(8,128)(2,1)S(1)} %gather_fusion.6), channel_id=1, source_target_pairs={{0,4},{4,8},{8,12},{12,16},{16,20},{20,24},{24,28},{1,5},{5,9},{9,... | collective-permute-start | bytes 393224 | tf_op jit(solution)/shard_map/ppermute | solution.py:15
  144.4 1.3 collective-permute-start.5
  145.7 1.8 collective-permute-done.4
  147.6 4.1 %collective-permute-done.5 = bf16[64,1024]{1,0:T(8,128)(2,1)S(1)} collective-permute-done((bf16[64,1024]{1,0:T(8,128)(2,1)S(1)}, bf16[64,1024]{1,0:T(8,128)(2,1)S(1)}, u32[]{:S(2)}, u32[]{:S(2)}) %collective-permute-start.5) | collective-permute-done | bytes 131104 | tf_op jit(solution)/shard_map/ppermute | solution.py:15
  151.7 2.6 all-gather.9.cloned.1.call-done
  154.3 1.3 pad_maximum_fusion.2
  155.6 3.6 %gather_fusion.8 = bf16[896,1024]{1,0:T(8,128)(2,1)S(1)} fusion(bf16[640,1024]{1,0:T(8,128)(2,1)S(1)} %pad_maximum_fusion.2, s32[1024]{0:T(1024)S(1)} %pad_clamp_fusion), kind=kCustom, calls=%fused_computation.8 | custom fusion | bytes 3673600 | tf_op jit(solution)/shard_map/gather | solution.py:48
  159.3 13.8 %reshape.130 = bf16[128,7,64,16]{3,2,1,0:T(8,128)(2,1)} reshape(bf16[896,1024]{1,0:T(8,128)(2,1)S(1)} %gather_fusion.8) | data formatting | bytes 3670016 | tf_op jit(solution)/shard_map/reshape | solution.py:48
  173.1 12.5 %constant_dynamic-update-slice_fusion = (bf16[128,5,64,16]{2,3,0,1:T(8,128)(2,1)}, bf16[128,16,64]{2,1,0:T(8,128)(2,1)S(1)}) fusion(bf16[128,5,64,16]{2,3,0,1:T(8,128)(2,1)} %get-tuple-element.10, bf16[128,7,64,16]{3,2,1,0:T(8,128)(2,1)} %reshape.130, bf16[128,7,64,64]{3,2,1,0:T(8,128)(2,1)} %copy.29), kind=kOutput, calls=%fused_computation.55 | convolution fusion | flops 117571584 | bytes 30146560 | tf_op jit(solution)/shard_map/rbij,rbjk->rik/dot_general | solution.py:49
  186.2 0.9 copy.44
  187.1 1.8 gather_fusion.9
  188.9 1.8 gather_fusion.10
  190.6 3.4 %collective-permute-start.6 = (bf16[64,1024]{1,0:T(8,128)(2,1)S(1)}, bf16[64,1024]{1,0:T(8,128)(2,1)S(1)}, u32[]{:S(2)}, u32[]{:S(2)}) collective-permute-start(bf16[64,1024]{1,0:T(8,128)(2,1)S(1)} %gather_fusion.9), channel_id=1, source_target_pairs={{0,4},{4,8},{8,12},{12,16},{16,20},{20,24},{24,28},{1,5},{5,9},{9,... | collective-permute-start | bytes 393224 | tf_op jit(solution)/shard_map/ppermute | solution.py:15
  194.0 1.5 collective-permute-start.7
  195.6 0.9 copy.56
  196.5 0.7 collective-permute-done.6
  197.2 4.1 %collective-permute-done.7 = bf16[64,1024]{1,0:T(8,128)(2,1)S(1)} collective-permute-done((bf16[64,1024]{1,0:T(8,128)(2,1)S(1)}, bf16[64,1024]{1,0:T(8,128)(2,1)S(1)}, u32[]{:S(2)}, u32[]{:S(2)}) %collective-permute-start.7) | collective-permute-done | bytes 131104 | tf_op jit(solution)/shard_map/ppermute | solution.py:15
  201.3 2.7 all-gather.11.cloned.1.call-done
  204.0 1.3 pad_maximum_fusion.3
  205.3 3.6 %gather_fusion.11 = bf16[896,1024]{1,0:T(8,128)(2,1)S(1)} fusion(bf16[640,1024]{1,0:T(8,128)(2,1)S(1)} %pad_maximum_fusion.3, s32[1024]{0:T(1024)S(1)} %pad_clamp_fusion), kind=kCustom, calls=%fused_computation.11 | custom fusion | bytes 3673600 | tf_op jit(solution)/shard_map/gather | solution.py:48
  208.9 13.8 %reshape.132 = bf16[128,7,64,16]{3,2,1,0:T(8,128)(2,1)} reshape(bf16[896,1024]{1,0:T(8,128)(2,1)S(1)} %gather_fusion.11) | data formatting | bytes 3670016 | tf_op jit(solution)/shard_map/reshape | solution.py:48
  222.7 12.5 %fusion.18 = bf16[128,5,64,16]{2,3,0,1:T(8,128)(2,1)} fusion(bf16[128,5,64,16]{2,3,0,1:T(8,128)(2,1)} %get-tuple-element.12, bf16[128,7,64,16]{3,2,1,0:T(8,128)(2,1)} %reshape.132, bf16[128,7,64,64]{3,2,1,0:T(8,128)(2,1)} %copy.29), kind=kOutput, calls=%fused_computation.39 | convolution fusion | flops 117571584 | bytes 29884416 | tf_op jit(solution)/shard_map/rbij,rbjk->rik/dot_general | solution.py:49
  235.3 4.7 %convert_element_type.36 = f32[128,5,64,16]{2,3,0,1:T(8,128)} convert(bf16[128,5,64,16]{2,3,0,1:T(8,128)(2,1)} %fusion.18) | non-fusion elementwise | flops 655360 | bytes 3932160 | tf_op jit(solution)/shard_map/convert_element_type | solution.py:25
  240.0 3.8 %fusion.19 = f32[5,16,5,16]{3,1,2,0:T(8,128)S(1)} fusion(bf16[128,5,64,16]{2,3,0,1:T(8,128)(2,1)S(1)} %copy-done.1), kind=kOutput, calls=%fused_computation.40 | convolution fusion | flops 104857600 | bytes 1336320 | tf_op jit(solution)/shard_map/rjia,rkic->jakc/dot_general | solution.py:52
  243.8 43.3 %psum.7 = f32[5,16,5,16]{3,1,2,0:T(8,128)S(1)} all-reduce(f32[5,16,5,16]{3,1,2,0:T(8,128)S(1)} %fusion.19), channel_id=1, replica_groups=mesh['space'=8,'sub'=4] {'space','sub'}, use_global_device_ids=true, to_apply=%region_0.0 | all-reduce | flops 6400 | bytes 51200 | tf_op jit(solution)/shard_map/psum | solution.py:53
  287.5 5.8 %cholesky.16 = f32[64,64]{1,0:T(8,128)S(1)} custom-call(f32[64,64]{1,0:T(8,128)S(1)} %fusion.26), custom_call_target="Cholesky" | custom-call | tf_op jit(solution)/shard_map/jit(cholesky)/cholesky | solution.py:23
  293.4 0.7 compare_reduce_fusion
  294.6 4.9 %custom-call.10 = f32[1,64,64]{1,2,0:T(8,128)S(1)} custom-call(f32[1,64,64]{2,1,0:T(8,128)S(1)} %fusion.24), custom_call_target="InvertDiagBlocksLowerTriangular" | custom-call | tf_op jit(solution)/shard_map/jit(_cho_solve)/triangular_solve | solution.py:24
  300.1 4.8 %fusion = f32[128,64,16,1]{1,2,0,3:T(8,128)S(1)} fusion(f32[4,16,16,1]{1,2,3,0:T(8,128)S(1)} %convolution_bitcast_fusion.4, f32[128,5,64,16]{2,3,0,1:T(8,128)} %convert_element_type.36), kind=kOutput, calls=%fused_computation.13 | convolution fusion | flops 101187584 | bytes 8916992 | tf_op jit(solution)/shard_map/rjia,jac->ric/dot_general | solution.py:29
  305.5 1.2 bitcast_subtract_fusion
  306.7 1.0 copy.60
  307.7 2.2 fusion.5
  309.9 1.7 copy.75
  311.6 1.0 copy.59
  (53 shorter events, 4.0 us)
Async XLA Ops:
  7.2 11.7 %copy-start = (bf16[128,1024]{1,0:T(8,128)(2,1)S(1)}, bf16[128,1024]{1,0:T(8,128)(2,1)}, u32[]{:S(2)}) copy-start(bf16[128,1024]{1,0:T(8,128)(2,1)} %param.4) | copy-start | bytes 786436
  7.2 11.4 %copy-start.10 = (s32[128,7]{0,1:T(8,128)S(1)}, s32[128,7]{0,1:T(8,128)}, u32[]{:S(2)}) copy-start(s32[128,7]{0,1:T(8,128)} %param.6) | copy-start | bytes 10756
  7.2 45.6 %all-gather.5.cloned.1.call-start = ((), (), s32[]{:S(2)}) async-start(), calls=%async_computation | async-start | bytes 1310720 | tf_op jit(solution)/shard_map/all_gather | solution.py:46
  7.9 96.7 %all-gather.7.cloned.1.call-start = ((), (), s32[]{:S(2)}) async-start(), calls=%async_computation.1 | async-start | bytes 1310720 | tf_op jit(solution)/shard_map/all_gather | solution.py:46
  10.6 42.1 %collective-permute-start = (bf16[64,1024]{1,0:T(8,128)(2,1)S(1)}, bf16[64,1024]{1,0:T(8,128)(2,1)S(1)}, u32[]{:S(2)}, u32[]{:S(2)}) collective-permute-start(bf16[64,1024]{1,0:T(8,128)(2,1)S(1)} %gather_fusion), channel_id=1, source_target_pairs={{0,4},{4,8},{8,12},{12,16},{16,20},{20,24},{24,28},{1,5},{5,9},{9,... | collective-permute-start | bytes 393224 | tf_op jit(solution)/shard_map/ppermute | solution.py:15
  17.2 35.5 %collective-permute-start.1 = (bf16[64,1024]{1,0:T(8,128)(2,1)S(1)}, bf16[64,1024]{1,0:T(8,128)(2,1)S(1)}, u32[]{:S(2)}, u32[]{:S(2)}) collective-permute-start(bf16[64,1024]{1,0:T(8,128)(2,1)S(1)} %gather_fusion.1), channel_id=1, source_target_pairs={{4,0},{8,4},{12,8},{16,12},{20,16},{24,20},{28,24},{5,1},{9,5},{13... | collective-permute-start | bytes 393224 | tf_op jit(solution)/shard_map/ppermute | solution.py:15
  51.7 1.0 copy-start.8
  84.1 16.8 %copy-start.2 = (bf16[128,16,64]{2,1,0:T(8,128)(2,1)}, bf16[128,16,64]{2,1,0:T(8,128)(2,1)S(1)}, u32[]{:S(2)}) copy-start(bf16[128,16,64]{2,1,0:T(8,128)(2,1)S(1)} %get-tuple-element.9) | copy-start | bytes 786436
  85.5 68.8 %all-gather.9.cloned.1.call-start = ((), (), s32[]{:S(2)}) async-start(), calls=%async_computation.2 | async-start | bytes 1310720 | tf_op jit(solution)/shard_map/all_gather | solution.py:46
  89.2 6.9 %collective-permute-start.2 = (bf16[64,1024]{1,0:T(8,128)(2,1)S(1)}, bf16[64,1024]{1,0:T(8,128)(2,1)S(1)}, u32[]{:S(2)}, u32[]{:S(2)}) collective-permute-start(bf16[64,1024]{1,0:T(8,128)(2,1)S(1)} %gather_fusion.3), channel_id=1, source_target_pairs={{0,4},{4,8},{8,12},{12,16},{16,20},{20,24},{24,28},{1,5},{5,9},{9,... | collective-permute-start | bytes 393224 | tf_op jit(solution)/shard_map/ppermute | solution.py:15
  93.6 7.3 %collective-permute-start.3 = (bf16[64,1024]{1,0:T(8,128)(2,1)S(1)}, bf16[64,1024]{1,0:T(8,128)(2,1)S(1)}, u32[]{:S(2)}, u32[]{:S(2)}) collective-permute-start(bf16[64,1024]{1,0:T(8,128)(2,1)S(1)} %gather_fusion.4), channel_id=1, source_target_pairs={{4,0},{8,4},{12,8},{16,12},{20,16},{24,20},{28,24},{5,1},{9,5},{13... | collective-permute-start | bytes 393224 | tf_op jit(solution)/shard_map/ppermute | solution.py:15
  135.9 15.7 %copy-start.4 = (bf16[128,16,64]{2,1,0:T(8,128)(2,1)}, bf16[128,16,64]{2,1,0:T(8,128)(2,1)S(1)}, u32[]{:S(2)}) copy-start(bf16[128,16,64]{2,1,0:T(8,128)(2,1)S(1)} %get-tuple-element.11) | copy-start | bytes 786436
  137.4 66.5 %all-gather.11.cloned.1.call-start = ((), (), s32[]{:S(2)}) async-start(), calls=%async_computation.3 | async-start | bytes 1310720 | tf_op jit(solution)/shard_map/all_gather | solution.py:46
  141.0 6.5 %collective-permute-start.4 = (bf16[64,1024]{1,0:T(8,128)(2,1)S(1)}, bf16[64,1024]{1,0:T(8,128)(2,1)S(1)}, u32[]{:S(2)}, u32[]{:S(2)}) collective-permute-start(bf16[64,1024]{1,0:T(8,128)(2,1)S(1)} %gather_fusion.6), channel_id=1, source_target_pairs={{0,4},{4,8},{8,12},{12,16},{16,20},{20,24},{24,28},{1,5},{5,9},{9,... | collective-permute-start | bytes 393224 | tf_op jit(solution)/shard_map/ppermute | solution.py:15
  144.4 7.2 %collective-permute-start.5 = (bf16[64,1024]{1,0:T(8,128)(2,1)S(1)}, bf16[64,1024]{1,0:T(8,128)(2,1)S(1)}, u32[]{:S(2)}, u32[]{:S(2)}) collective-permute-start(bf16[64,1024]{1,0:T(8,128)(2,1)S(1)} %gather_fusion.7), channel_id=1, source_target_pairs={{4,0},{8,4},{12,8},{16,12},{20,16},{24,20},{28,24},{5,1},{9,5},{13... | collective-permute-start | bytes 393224 | tf_op jit(solution)/shard_map/ppermute | solution.py:15
  185.6 15.7 %copy-start.6 = (bf16[128,16,64]{2,1,0:T(8,128)(2,1)}, bf16[128,16,64]{2,1,0:T(8,128)(2,1)S(1)}, u32[]{:S(2)}) copy-start(bf16[128,16,64]{2,1,0:T(8,128)(2,1)S(1)} %get-tuple-element.13) | copy-start | bytes 786436
  190.6 6.5 %collective-permute-start.6 = (bf16[64,1024]{1,0:T(8,128)(2,1)S(1)}, bf16[64,1024]{1,0:T(8,128)(2,1)S(1)}, u32[]{:S(2)}, u32[]{:S(2)}) collective-permute-start(bf16[64,1024]{1,0:T(8,128)(2,1)S(1)} %gather_fusion.9), channel_id=1, source_target_pairs={{0,4},{4,8},{8,12},{12,16},{16,20},{20,24},{24,28},{1,5},{5,9},{9,... | collective-permute-start | bytes 393224 | tf_op jit(solution)/shard_map/ppermute | solution.py:15
  194.0 7.2 %collective-permute-start.7 = (bf16[64,1024]{1,0:T(8,128)(2,1)S(1)}, bf16[64,1024]{1,0:T(8,128)(2,1)S(1)}, u32[]{:S(2)}, u32[]{:S(2)}) collective-permute-start(bf16[64,1024]{1,0:T(8,128)(2,1)S(1)} %gather_fusion.10), channel_id=1, source_target_pairs={{4,0},{8,4},{12,8},{16,12},{20,16},{24,20},{28,24},{5,1},{9,5},{13... | collective-permute-start | bytes 393224 | tf_op jit(solution)/shard_map/ppermute | solution.py:15
  235.3 4.7 %copy-start.1 = (bf16[128,5,64,16]{2,3,0,1:T(8,128)(2,1)S(1)}, bf16[128,5,64,16]{2,3,0,1:T(8,128)(2,1)}, u32[]{:S(2)}) copy-start(bf16[128,5,64,16]{2,3,0,1:T(8,128)(2,1)} %fusion.18) | copy-start | bytes 3932164
  304.9 2.8 copy-start.3
  304.9 2.8 copy-start.5
  304.9 2.8 copy-start.7
  305.5 2.2 copy-start.9
Sparse Core Ops, SparseCore 0:
  9.6 19.4 all-gather.4
  85.6 18.9 all-gather.6
  137.5 16.7 all-gather.8
  187.2 16.7 all-gather.10
where the time goes:
time: 321 us; the launch traced here: 319 us
  local copies, waits for them, and re-layouts  128 us (40%)
  matrix products  61.5 us (19%)
  blocking collectives  43.3 us (13%)
  waiting for transfers between devices  26.3 us (8%)
  other arithmetic  24.1 us (8%)
  starting transfers between devices  21.8 us (7%)
  between operations  14.2 us (4%)
    reshape x4, local copies, waits for them, and re-layouts, on_device(): picked = extended[columns].reshape(rows, NNZ, BS, NRHS)  55.2 us
    dot_general x4, matrix products, on_device(): jnp.einsum('rbij,rbjk->rik', mats, picked, preferred_element_type=jnp.flo...  50.1 us
    psum x1, blocking collectives, on_device(): gram = lax.psum(partial_value, ('space', 'sub'))  43.3 us
    ppermute x8, starting transfers between devices, shifted(): lax.ppermute(value, axis, [(source, source + steps) for source in range(i...  21.6 us
    reshape x1, local copies, waits for them, and re-layouts, on_device(): mats = blocks.reshape(rows, NNZ, BS, BS)  21.2 us
    ppermute x8, waiting for transfers between devices, shifted(): lax.ppermute(value, axis, [(source, source + steps) for source in range(i...  16.5 us
    gather x4, local copies, waits for them, and re-layouts, on_device(): picked = extended[columns].reshape(rows, NNZ, BS, NRHS)  14.4 us
    unnamed x27, local copies, waits for them, and re-layouts  14.1 us
  transfers between devices with their start and end apart: 12, of which 9 were waited for; matrix products, arithmetic and copies ran while one was open for 16% of the time, Pallas kernels for 0%

commit v1 on v0

--- a/solution.py
+++ b/solution.py
@@ -7,6 +7,7 @@
 NRHS = 16
 NNZ = 7
 S = 4
+_part_slabs = lambda my_tile: jax.lax.psum(jax.lax.psum(my_tile, "sub"), "space")
 
 
 def shifted(value, axis, steps):
@@ -50,7 +51,7 @@
         basis.append(nxt.astype(jnp.bfloat16).reshape(rows, BS * NRHS))
     stack = jnp.stack(basis, axis=1).reshape(rows, S + 1, BS, NRHS)
     partial_value = jnp.einsum("rjia,rkic->jakc", stack, stack, preferred_element_type=jnp.float32)
-    gram = lax.psum(partial_value, ("space", "sub"))
+    gram = _part_slabs(partial_value)
     return finish(rhs, stack, gram)
 
 

time: 321 us -> 330 us (1.028)
  blocking collectives: 43.3 us -> 53.2 us
    psum x1 -> x2, blocking collectives: 43.3 us -> 53.2 us  [the longest x1 40.5 us: jax.lax.psum(jax.lax.psum(my_tile, 'sub'), 'space')]
  transfers between devices with their start and end apart: 12 -> 12, of which waited for: 9 -> 9; matrix products, arithmetic and copies ran while one was open for 16% -> 15% of each run, Pallas kernels for 0% -> 0%
where the time goes in v1:
time: 330 us; the launch traced here: 329 us
  local copies, waits for them, and re-layouts  128 us (39%)
  matrix products  61.5 us (19%)
  blocking collectives  53.2 us (16%)
  waiting for transfers between devices  26.3 us (8%)
  other arithmetic  24.3 us (7%)
  starting transfers between devices  21.8 us (7%)
  between operations  14.2 us (4%)
    reshape x4, local copies, waits for them, and re-layouts, on_device(): picked = extended[columns].reshape(rows, NNZ, BS, NRHS)  54.9 us
    dot_general x4, matrix products, on_device(): jnp.einsum('rbij,rbjk->rik', mats, picked, preferred_element_type=jnp.flo...  50.1 us
    psum x1, blocking collectives, jax.lax.psum(jax.lax.psum(my_tile, 'sub'), 'space')  40.5 us
    ppermute x8, starting transfers between devices, shifted(): lax.ppermute(value, axis, [(source, source + steps) for source in range(i...  21.6 us
    reshape x1, local copies, waits for them, and re-layouts, on_device(): mats = blocks.reshape(rows, NNZ, BS, BS)  21.2 us
    ppermute x8, waiting for transfers between devices, shifted(): lax.ppermute(value, axis, [(source, source + steps) for source in range(i...  16.5 us
    gather x4, local copies, waits for them, and re-layouts, on_device(): picked = extended[columns].reshape(rows, NNZ, BS, NRHS)  14.4 us
    unnamed x27, local copies, waits for them, and re-layouts  14.1 us
  transfers between devices with their start and end apart: 12, of which 9 were waited for; matrix products, arithmetic and copies ran while one was open for 15% of the time, Pallas kernels for 0%

profile of v1, /device:TPU:0, one launch (start us, length us, event | category | flops | bytes accessed | tf_op | source)
XLA Modules:
  0.0 329.0 jit_solution(17564537248717988769)
XLA Ops:
  7.2 0.7 all-gather.5.cloned.1.call-update
  8.0 0.8 fusion.27
  8.8 1.8 gather_fusion
  10.6 4.9 %collective-permute-start = (bf16[64,1024]{1,0:T(8,128)(2,1)S(1)}, bf16[64,1024]{1,0:T(8,128)(2,1)S(1)}, u32[]{:S(2)}, u32[]{:S(2)}) collective-permute-start(bf16[64,1024]{1,0:T(8,128)(2,1)S(1)} %gather_fusion), channel_id=1, source_target_pairs={{0,4},{4,8},{8,12},{12,16},{16,20},{20,24},{24,28},{1,5},{5,9},{9,... | collective-permute-start | bytes 393224 | tf_op jit(solution)/shard_map/ppermute | solution.py:16
  15.5 1.8 gather_fusion.1
  17.2 1.3 collective-permute-start.1
  19.1 10.9 %copy.27 = bf16[128,7,4096]{0,2,1:T(8,128)(2,1)} copy(bf16[128,7,4096]{2,0,1:T(8,128)(2,1)} %param.5) | data formatting | bytes 14680064 | tf_op args[1]
  30.0 21.2 %copy.29 = bf16[128,7,64,64]{3,2,1,0:T(8,128)(2,1)} copy(bf16[128,7,64,64]{0,3,2,1:T(8,128)(2,1)} %bitcast.114) | data formatting | bytes 14680064 | tf_op jit(solution)/shard_map/reshape | solution.py:40
  51.8 0.9 constant_dynamic-update-slice_fusion.3
  52.8 1.3 pad_maximum_fusion
  54.1 3.6 %gather_fusion.2 = bf16[896,1024]{1,0:T(8,128)(2,1)S(1)} fusion(bf16[640,1024]{1,0:T(8,128)(2,1)S(1)} %pad_maximum_fusion, s32[1024]{0:T(1024)S(1)} %pad_clamp_fusion), kind=kCustom, calls=%fused_computation.2 | custom fusion | bytes 3673600 | tf_op jit(solution)/shard_map/gather | solution.py:49
  57.8 13.7 %reshape.125 = bf16[128,7,64,16]{3,2,1,0:T(8,128)(2,1)} reshape(bf16[896,1024]{1,0:T(8,128)(2,1)S(1)} %gather_fusion.2) | data formatting | bytes 3670016 | tf_op jit(solution)/shard_map/reshape | solution.py:49
  71.5 12.5 %constant_dynamic-update-slice_fusion.2 = (bf16[128,5,64,16]{2,3,0,1:T(8,128)(2,1)}, bf16[128,16,64]{2,1,0:T(8,128)(2,1)S(1)}) fusion(bf16[128,5,64,16]{2,3,0,1:T(8,128)(2,1)} %constant_dynamic-update-slice_fusion.3, bf16[128,7,64,16]{3,2,1,0:T(8,128)(2,1)} %reshape.125, bf16[128,7,64,64]{3,2,1,0:T(8,128)(2,1)} %copy.29), kind=kOutput, calls=%fused_computation.57 | convolution fusion | flops 117571584 | bytes 30146560 | tf_op jit(solution)/shard_map/rbij,rbjk->rik/dot_general | solution.py:50
  84.6 0.9 copy.31
  85.5 1.8 gather_fusion.3
  87.3 1.8 gather_fusion.4
  89.1 4.4 %collective-permute-start.2 = (bf16[64,1024]{1,0:T(8,128)(2,1)S(1)}, bf16[64,1024]{1,0:T(8,128)(2,1)S(1)}, u32[]{:S(2)}, u32[]{:S(2)}) collective-permute-start(bf16[64,1024]{1,0:T(8,128)(2,1)S(1)} %gather_fusion.3), channel_id=1, source_target_pairs={{0,4},{4,8},{8,12},{12,16},{16,20},{20,24},{24,28},{1,5},{5,9},{9,... | collective-permute-start | bytes 393224 | tf_op jit(solution)/shard_map/ppermute | solution.py:16
  93.5 1.5 collective-permute-start.3
  95.0 1.0 collective-permute-done.2
  96.0 4.8 %collective-permute-done.3 = bf16[64,1024]{1,0:T(8,128)(2,1)S(1)} collective-permute-done((bf16[64,1024]{1,0:T(8,128)(2,1)S(1)}, bf16[64,1024]{1,0:T(8,128)(2,1)S(1)}, u32[]{:S(2)}, u32[]{:S(2)}) %collective-permute-start.3) | collective-permute-done | bytes 131104 | tf_op jit(solution)/shard_map/ppermute | solution.py:16
  100.8 3.8 %all-gather.7.cloned.1.call-done = bf16[512,1024]{1,0:T(8,128)(2,1)} async-done(((bf16[128,1024]{1,0:T(8,128)(2,1)}), bf16[512,1024]{1,0:T(8,128)(2,1)}) %all-gather.7.cloned.1.call-update) | async-done | bytes 1048592 | tf_op jit(solution)/shard_map/all_gather | solution.py:47
  104.6 1.3 pad_maximum_fusion.1
  105.9 3.6 %gather_fusion.5 = bf16[896,1024]{1,0:T(8,128)(2,1)S(1)} fusion(bf16[640,1024]{1,0:T(8,128)(2,1)S(1)} %pad_maximum_fusion.1, s32[1024]{0:T(1024)S(1)} %pad_clamp_fusion), kind=kCustom, calls=%fused_computation.5 | custom fusion | bytes 3673600 | tf_op jit(solution)/shard_map/gather | solution.py:49
  109.6 13.7 %reshape.128 = bf16[128,7,64,16]{3,2,1,0:T(8,128)(2,1)} reshape(bf16[896,1024]{1,0:T(8,128)(2,1)S(1)} %gather_fusion.5) | data formatting | bytes 3670016 | tf_op jit(solution)/shard_map/reshape | solution.py:49
  123.3 12.5 %constant_dynamic-update-slice_fusion.1 = (bf16[128,5,64,16]{2,3,0,1:T(8,128)(2,1)}, bf16[128,16,64]{2,1,0:T(8,128)(2,1)S(1)}) fusion(bf16[128,5,64,16]{2,3,0,1:T(8,128)(2,1)} %get-tuple-element.8, bf16[128,7,64,16]{3,2,1,0:T(8,128)(2,1)} %reshape.128, bf16[128,7,64,64]{3,2,1,0:T(8,128)(2,1)} %copy.29), kind=kOutput, calls=%fused_computation.56 | convolution fusion | flops 117571584 | bytes 30146560 | tf_op jit(solution)/shard_map/rbij,rbjk->rik/dot_general | solution.py:50
  136.4 0.9 copy.37
  137.3 1.8 gather_fusion.6
  139.1 1.8 gather_fusion.7
  140.9 3.4 %collective-permute-start.4 = (bf16[64,1024]{1,0:T(8,128)(2,1)S(1)}, bf16[64,1024]{1,0:T(8,128)(2,1)S(1)}, u32[]{:S(2)}, u32[]{:S(2)}) collective-permute-start(bf16[64,1024]{1,0:T(8,128)(2,1)S(1)} %gather_fusion.6), channel_id=1, source_target_pairs={{0,4},{4,8},{8,12},{12,16},{16,20},{20,24},{24,28},{1,5},{5,9},{9,... | collective-permute-start | bytes 393224 | tf_op jit(solution)/shard_map/ppermute | solution.py:16
  144.3 1.3 collective-permute-start.5
  145.6 1.8 collective-permute-done.4
  147.4 4.1 %collective-permute-done.5 = bf16[64,1024]{1,0:T(8,128)(2,1)S(1)} collective-permute-done((bf16[64,1024]{1,0:T(8,128)(2,1)S(1)}, bf16[64,1024]{1,0:T(8,128)(2,1)S(1)}, u32[]{:S(2)}, u32[]{:S(2)}) %collective-permute-start.5) | collective-permute-done | bytes 131104 | tf_op jit(solution)/shard_map/ppermute | solution.py:16
  151.5 2.6 all-gather.9.cloned.1.call-done
  154.1 1.3 pad_maximum_fusion.2
  155.5 3.6 %gather_fusion.8 = bf16[896,1024]{1,0:T(8,128)(2,1)S(1)} fusion(bf16[640,1024]{1,0:T(8,128)(2,1)S(1)} %pad_maximum_fusion.2, s32[1024]{0:T(1024)S(1)} %pad_clamp_fusion), kind=kCustom, calls=%fused_computation.8 | custom fusion | bytes 3673600 | tf_op jit(solution)/shard_map/gather | solution.py:49
  159.1 13.7 %reshape.130 = bf16[128,7,64,16]{3,2,1,0:T(8,128)(2,1)} reshape(bf16[896,1024]{1,0:T(8,128)(2,1)S(1)} %gather_fusion.8) | data formatting | bytes 3670016 | tf_op jit(solution)/shard_map/reshape | solution.py:49
  172.8 12.5 %constant_dynamic-update-slice_fusion = (bf16[128,5,64,16]{2,3,0,1:T(8,128)(2,1)}, bf16[128,16,64]{2,1,0:T(8,128)(2,1)S(1)}) fusion(bf16[128,5,64,16]{2,3,0,1:T(8,128)(2,1)} %get-tuple-element.10, bf16[128,7,64,16]{3,2,1,0:T(8,128)(2,1)} %reshape.130, bf16[128,7,64,64]{3,2,1,0:T(8,128)(2,1)} %copy.29), kind=kOutput, calls=%fused_computation.55 | convolution fusion | flops 117571584 | bytes 30146560 | tf_op jit(solution)/shard_map/rbij,rbjk->rik/dot_general | solution.py:50
  186.0 0.8 copy.44
  186.8 1.8 gather_fusion.9
  188.6 1.8 gather_fusion.10
  190.4 3.4 %collective-permute-start.6 = (bf16[64,1024]{1,0:T(8,128)(2,1)S(1)}, bf16[64,1024]{1,0:T(8,128)(2,1)S(1)}, u32[]{:S(2)}, u32[]{:S(2)}) collective-permute-start(bf16[64,1024]{1,0:T(8,128)(2,1)S(1)} %gather_fusion.9), channel_id=1, source_target_pairs={{0,4},{4,8},{8,12},{12,16},{16,20},{20,24},{24,28},{1,5},{5,9},{9,... | collective-permute-start | bytes 393224 | tf_op jit(solution)/shard_map/ppermute | solution.py:16
  193.8 1.5 collective-permute-start.7
  195.3 0.9 copy.56
  196.3 0.7 collective-permute-done.6
  196.9 4.1 %collective-permute-done.7 = bf16[64,1024]{1,0:T(8,128)(2,1)S(1)} collective-permute-done((bf16[64,1024]{1,0:T(8,128)(2,1)S(1)}, bf16[64,1024]{1,0:T(8,128)(2,1)S(1)}, u32[]{:S(2)}, u32[]{:S(2)}) %collective-permute-start.7) | collective-permute-done | bytes 131104 | tf_op jit(solution)/shard_map/ppermute | solution.py:16
  201.1 2.7 all-gather.11.cloned.1.call-done
  203.7 1.3 pad_maximum_fusion.3
  205.1 3.6 %gather_fusion.11 = bf16[896,1024]{1,0:T(8,128)(2,1)S(1)} fusion(bf16[640,1024]{1,0:T(8,128)(2,1)S(1)} %pad_maximum_fusion.3, s32[1024]{0:T(1024)S(1)} %pad_clamp_fusion), kind=kCustom, calls=%fused_computation.11 | custom fusion | bytes 3673600 | tf_op jit(solution)/shard_map/gather | solution.py:49
  208.7 13.7 %reshape.132 = bf16[128,7,64,16]{3,2,1,0:T(8,128)(2,1)} reshape(bf16[896,1024]{1,0:T(8,128)(2,1)S(1)} %gather_fusion.11) | data formatting | bytes 3670016 | tf_op jit(solution)/shard_map/reshape | solution.py:49
  222.4 12.5 %fusion.18 = bf16[128,5,64,16]{2,3,0,1:T(8,128)(2,1)} fusion(bf16[128,5,64,16]{2,3,0,1:T(8,128)(2,1)} %get-tuple-element.12, bf16[128,7,64,16]{3,2,1,0:T(8,128)(2,1)} %reshape.132, bf16[128,7,64,64]{3,2,1,0:T(8,128)(2,1)} %copy.29), kind=kOutput, calls=%fused_computation.39 | convolution fusion | flops 117571584 | bytes 29884416 | tf_op jit(solution)/shard_map/rbij,rbjk->rik/dot_general | solution.py:50
  234.9 4.7 %convert_element_type.36 = f32[128,5,64,16]{2,3,0,1:T(8,128)} convert(bf16[128,5,64,16]{2,3,0,1:T(8,128)(2,1)} %fusion.18) | non-fusion elementwise | flops 655360 | bytes 3932160 | tf_op jit(solution)/shard_map/convert_element_type | solution.py:26
  239.6 3.8 %fusion.19 = f32[5,16,5,16]{3,1,2,0:T(8,128)S(1)} fusion(bf16[128,5,64,16]{2,3,0,1:T(8,128)(2,1)S(1)} %copy-done.1), kind=kOutput, calls=%fused_computation.40 | convolution fusion | flops 104857600 | bytes 1336320 | tf_op jit(solution)/shard_map/rjia,rkic->jakc/dot_general | solution.py:53
  243.5 12.7 %psum.14 = f32[5,16,5,16]{3,1,2,0:T(8,128)S(1)} all-reduce(f32[5,16,5,16]{3,1,2,0:T(8,128)S(1)} %fusion.19), channel_id=1, replica_groups=mesh['space'=8,'sub'=4] {'sub'}, use_global_device_ids=true, to_apply=%region_0.0 | all-reduce | flops 6400 | bytes 51200 | tf_op jit(solution)/shard_map/psum | solution.py:10
  256.2 40.5 %psum.15 = f32[5,16,5,16]{3,1,2,0:T(8,128)S(1)} all-reduce(f32[5,16,5,16]{3,1,2,0:T(8,128)S(1)} %psum.14), channel_id=1, replica_groups=mesh['space'=8,'sub'=4] {'space'}, use_global_device_ids=true, to_apply=%region_1.0 | all-reduce | flops 6400 | bytes 51200 | tf_op jit(solution)/shard_map/psum | solution.py:10
  297.1 5.8 %cholesky.16 = f32[64,64]{1,0:T(8,128)S(1)} custom-call(f32[64,64]{1,0:T(8,128)S(1)} %fusion.26), custom_call_target="Cholesky" | custom-call | tf_op jit(solution)/shard_map/jit(cholesky)/cholesky | solution.py:24
  303.0 0.7 compare_reduce_fusion
  303.7 0.7 fusion.24
  304.4 4.9 %custom-call.10 = f32[1,64,64]{1,2,0:T(8,128)S(1)} custom-call(f32[1,64,64]{2,1,0:T(8,128)S(1)} %fusion.24), custom_call_target="InvertDiagBlocksLowerTriangular" | custom-call | tf_op jit(solution)/shard_map/jit(_cho_solve)/triangular_solve | solution.py:25
  309.9 4.8 %fusion = f32[128,64,16,1]{1,2,0,3:T(8,128)S(1)} fusion(f32[4,16,16,1]{1,2,3,0:T(8,128)S(1)} %convolution_bitcast_fusion.4, f32[128,5,64,16]{2,3,0,1:T(8,128)} %convert_element_type.36), kind=kOutput, calls=%fused_computation.13 | convolution fusion | flops 101187584 | bytes 8916992 | tf_op jit(solution)/shard_map/rjia,jac->ric/dot_general | solution.py:30
  315.3 1.2 bitcast_subtract_fusion
  316.5 1.0 copy.60
  317.5 2.2 fusion.5
  319.7 1.7 copy.75
  321.4 1.0 copy.59
  (54 shorter events, 4.6 us)
Async XLA Ops:
  7.2 11.7 %copy-start = (bf16[128,1024]{1,0:T(8,128)(2,1)S(1)}, bf16[128,1024]{1,0:T(8,128)(2,1)}, u32[]{:S(2)}) copy-start(bf16[128,1024]{1,0:T(8,128)(2,1)} %param.4) | copy-start | bytes 786436
  7.2 11.4 %copy-start.10 = (s32[128,7]{0,1:T(8,128)S(1)}, s32[128,7]{0,1:T(8,128)}, u32[]{:S(2)}) copy-start(s32[128,7]{0,1:T(8,128)} %param.6) | copy-start | bytes 10756
  7.2 45.6 %all-gather.5.cloned.1.call-start = ((), (), s32[]{:S(2)}) async-start(), calls=%async_computation | async-start | bytes 1310720 | tf_op jit(solution)/shard_map/all_gather | solution.py:47
  7.9 96.7 %all-gather.7.cloned.1.call-start = ((), (), s32[]{:S(2)}) async-start(), calls=%async_computation.1 | async-start | bytes 1310720 | tf_op jit(solution)/shard_map/all_gather | solution.py:47
  10.6 42.1 %collective-permute-start = (bf16[64,1024]{1,0:T(8,128)(2,1)S(1)}, bf16[64,1024]{1,0:T(8,128)(2,1)S(1)}, u32[]{:S(2)}, u32[]{:S(2)}) collective-permute-start(bf16[64,1024]{1,0:T(8,128)(2,1)S(1)} %gather_fusion), channel_id=1, source_target_pairs={{0,4},{4,8},{8,12},{12,16},{16,20},{20,24},{24,28},{1,5},{5,9},{9,... | collective-permute-start | bytes 393224 | tf_op jit(solution)/shard_map/ppermute | solution.py:16
  17.2 35.5 %collective-permute-start.1 = (bf16[64,1024]{1,0:T(8,128)(2,1)S(1)}, bf16[64,1024]{1,0:T(8,128)(2,1)S(1)}, u32[]{:S(2)}, u32[]{:S(2)}) collective-permute-start(bf16[64,1024]{1,0:T(8,128)(2,1)S(1)} %gather_fusion.1), channel_id=1, source_target_pairs={{4,0},{8,4},{12,8},{16,12},{20,16},{24,20},{28,24},{5,1},{9,5},{13... | collective-permute-start | bytes 393224 | tf_op jit(solution)/shard_map/ppermute | solution.py:16
  51.8 1.0 copy-start.8
  84.0 16.8 %copy-start.2 = (bf16[128,16,64]{2,1,0:T(8,128)(2,1)}, bf16[128,16,64]{2,1,0:T(8,128)(2,1)S(1)}, u32[]{:S(2)}) copy-start(bf16[128,16,64]{2,1,0:T(8,128)(2,1)S(1)} %get-tuple-element.9) | copy-start | bytes 786436
  85.5 68.7 %all-gather.9.cloned.1.call-start = ((), (), s32[]{:S(2)}) async-start(), calls=%async_computation.2 | async-start | bytes 1310720 | tf_op jit(solution)/shard_map/all_gather | solution.py:47
  89.1 6.9 %collective-permute-start.2 = (bf16[64,1024]{1,0:T(8,128)(2,1)S(1)}, bf16[64,1024]{1,0:T(8,128)(2,1)S(1)}, u32[]{:S(2)}, u32[]{:S(2)}) collective-permute-start(bf16[64,1024]{1,0:T(8,128)(2,1)S(1)} %gather_fusion.3), channel_id=1, source_target_pairs={{0,4},{4,8},{8,12},{12,16},{16,20},{20,24},{24,28},{1,5},{5,9},{9,... | collective-permute-start | bytes 393224 | tf_op jit(solution)/shard_map/ppermute | solution.py:16
  93.5 7.3 %collective-permute-start.3 = (bf16[64,1024]{1,0:T(8,128)(2,1)S(1)}, bf16[64,1024]{1,0:T(8,128)(2,1)S(1)}, u32[]{:S(2)}, u32[]{:S(2)}) collective-permute-start(bf16[64,1024]{1,0:T(8,128)(2,1)S(1)} %gather_fusion.4), channel_id=1, source_target_pairs={{4,0},{8,4},{12,8},{16,12},{20,16},{24,20},{28,24},{5,1},{9,5},{13... | collective-permute-start | bytes 393224 | tf_op jit(solution)/shard_map/ppermute | solution.py:16
  135.8 15.7 %copy-start.4 = (bf16[128,16,64]{2,1,0:T(8,128)(2,1)}, bf16[128,16,64]{2,1,0:T(8,128)(2,1)S(1)}, u32[]{:S(2)}) copy-start(bf16[128,16,64]{2,1,0:T(8,128)(2,1)S(1)} %get-tuple-element.11) | copy-start | bytes 786436
  137.3 66.5 %all-gather.11.cloned.1.call-start = ((), (), s32[]{:S(2)}) async-start(), calls=%async_computation.3 | async-start | bytes 1310720 | tf_op jit(solution)/shard_map/all_gather | solution.py:47
  140.9 6.5 %collective-permute-start.4 = (bf16[64,1024]{1,0:T(8,128)(2,1)S(1)}, bf16[64,1024]{1,0:T(8,128)(2,1)S(1)}, u32[]{:S(2)}, u32[]{:S(2)}) collective-permute-start(bf16[64,1024]{1,0:T(8,128)(2,1)S(1)} %gather_fusion.6), channel_id=1, source_target_pairs={{0,4},{4,8},{8,12},{12,16},{16,20},{20,24},{24,28},{1,5},{5,9},{9,... | collective-permute-start | bytes 393224 | tf_op jit(solution)/shard_map/ppermute | solution.py:16
  144.3 7.2 %collective-permute-start.5 = (bf16[64,1024]{1,0:T(8,128)(2,1)S(1)}, bf16[64,1024]{1,0:T(8,128)(2,1)S(1)}, u32[]{:S(2)}, u32[]{:S(2)}) collective-permute-start(bf16[64,1024]{1,0:T(8,128)(2,1)S(1)} %gather_fusion.7), channel_id=1, source_target_pairs={{4,0},{8,4},{12,8},{16,12},{20,16},{24,20},{28,24},{5,1},{9,5},{13... | collective-permute-start | bytes 393224 | tf_op jit(solution)/shard_map/ppermute | solution.py:16
  185.4 15.7 %copy-start.6 = (bf16[128,16,64]{2,1,0:T(8,128)(2,1)}, bf16[128,16,64]{2,1,0:T(8,128)(2,1)S(1)}, u32[]{:S(2)}) copy-start(bf16[128,16,64]{2,1,0:T(8,128)(2,1)S(1)} %get-tuple-element.13) | copy-start | bytes 786436
  190.4 6.5 %collective-permute-start.6 = (bf16[64,1024]{1,0:T(8,128)(2,1)S(1)}, bf16[64,1024]{1,0:T(8,128)(2,1)S(1)}, u32[]{:S(2)}, u32[]{:S(2)}) collective-permute-start(bf16[64,1024]{1,0:T(8,128)(2,1)S(1)} %gather_fusion.9), channel_id=1, source_target_pairs={{0,4},{4,8},{8,12},{12,16},{16,20},{20,24},{24,28},{1,5},{5,9},{9,... | collective-permute-start | bytes 393224 | tf_op jit(solution)/shard_map/ppermute | solution.py:16
  193.8 7.2 %collective-permute-start.7 = (bf16[64,1024]{1,0:T(8,128)(2,1)S(1)}, bf16[64,1024]{1,0:T(8,128)(2,1)S(1)}, u32[]{:S(2)}, u32[]{:S(2)}) collective-permute-start(bf16[64,1024]{1,0:T(8,128)(2,1)S(1)} %gather_fusion.10), channel_id=1, source_target_pairs={{4,0},{8,4},{12,8},{16,12},{20,16},{24,20},{28,24},{5,1},{9,5},{13... | collective-permute-start | bytes 393224 | tf_op jit(solution)/shard_map/ppermute | solution.py:16
  234.9 4.7 %copy-start.1 = (bf16[128,5,64,16]{2,3,0,1:T(8,128)(2,1)S(1)}, bf16[128,5,64,16]{2,3,0,1:T(8,128)(2,1)}, u32[]{:S(2)}) copy-start(bf16[128,5,64,16]{2,3,0,1:T(8,128)(2,1)} %fusion.18) | copy-start | bytes 3932164
  314.7 2.8 copy-start.3
  314.8 2.8 copy-start.5
  314.8 2.8 copy-start.7
  315.3 2.2 copy-start.9
Sparse Core Ops, SparseCore 0:
  9.6 19.4 all-gather.4
  85.6 18.9 all-gather.6
  137.4 16.7 all-gather.8
  187.0 16.7 all-gather.10
